TPU v7x, 32 devices: a whole 2x2x4 slice. The times are simulated.
32 devices in a mesh: seq: 8 (over z, core), batch: 4 (over y, x).
Axes of the slice: x: 2, y: 2, z: 4, core: 2. Of those that a mesh axis runs over, the one named last changes fastest.
Arguments:
- x_short: bfloat16 [8, 1024, 768], P('batch', 'seq'), may hold values from -6 to 6
- x_long: bfloat16 [8, 2048, 768], P('batch', 'seq'), may hold values from -6 to 6
- lengths: int32 [2, 8], P(None, 'batch'), may hold values from 256 to 2048, as said below
- cot_short: bfloat16 [8, 1024, 768], P('batch', 'seq'), may hold values from -6 to 6
- cot_long: bfloat16 [8, 2048, 768], P('batch', 'seq'), may hold values from -6 to 6
- w_qkv: bfloat16 [768, 2304], P(('seq', 'batch')), may hold values from -0.21875 to 0.21875
- w_out: bfloat16 [768, 768], P(('seq', 'batch')), may hold values from -1.25 to 1.25
- w_up: bfloat16 [768, 3072], P(('seq', 'batch')), may hold values from -0.21875 to 0.21875
- w_down: bfloat16 [3072, 768], P(('seq', 'batch')), may hold values from -0.109375 to 0.109375
- conv_kernel: bfloat16 [3, 2304], P(None, ('seq', 'batch')), may hold values from -3 to 3
- norm_params: bfloat16 [4, 768], P(None, ('seq', 'batch')), may hold values from -1.2 to 1.4
Outputs:
- y_short: bfloat16 [8, 1024, 768], P('batch', 'seq')
- y_long: bfloat16 [8, 2048, 768], P('batch', 'seq')
- dx_short: float32 [8, 1024, 768], P('batch', 'seq')
- dx_long: float32 [8, 2048, 768], P('batch', 'seq')
- grad_w_qkv: float32 [768, 2304], P(('seq', 'batch'))
- grad_w_out: float32 [768, 768], P(('seq', 'batch'))
- grad_w_up: float32 [768, 3072], P(('seq', 'batch'))
- grad_w_down: float32 [3072, 768], P(('seq', 'batch'))
- grad_conv_kernel: float32 [3, 2304], P(None, ('seq', 'batch'))
- grad_norm_params: float32 [4, 768], P(None, ('seq', 'batch'))
Inputs may be any that keep to these rules, and one draw needn't show every extreme that they name: Row 0 holds the lengths of the short sub-batch's sequences, the rest of each 1024-position slot being padding; row 1 those of the long sub-batch, in 2048-position slots. In each row, of the 2 sequences at one index of batch, one fills its whole slot and the other holds a quarter of its slot or more.
All inputs are finite; a program needn't handle non-finite values.
Results may differ from a plain program's by a relative error of at most 0.015.
The roundings to bfloat16 on the way count: a program that leaves them out, or rounds other values in their place, can miss the bound.
Values may be sent and summed in bfloat16 or wider, within the bound.
A program may use at most 320 MiB of HBM per device.

v0:
```python
import functools

import jax
import jax.numpy as jnp
from jax import lax
from jax.experimental import pallas as pl
from jax.experimental.pallas import tpu as pltpu
from jax.sharding import PartitionSpec as P

EPS = 1e-05
NEG_FILL = -1e30
HEAD_DIM = 64
LANES = 128
TRIPLE = 3 * LANES
TILE = 256
PAD = 16
MESH = pl.DeviceIdType.MESH
F32 = jnp.float32
BF16 = jnp.bfloat16
DMA = pltpu.SemaphoreType.DMA


def dot_nn(left, right):
    return lax.dot_general(left, right, (((1,), (0,)), ((), ())), preferred_element_type=F32)


def dot_nt(left, right):
    return lax.dot_general(left, right, (((1,), (1,)), ((), ())), preferred_element_type=F32)


def dot_tn(left, right):
    return lax.dot_general(left, right, (((0,), (0,)), ((), ())), preferred_element_type=F32)


def params_of(limit=60, **more):
    return pltpu.CompilerParams(vmem_limit_bytes=limit * 2**20, **more)


def vmem():
    return pl.BlockSpec(memory_space=pltpu.VMEM)


def smem():
    return pl.BlockSpec(memory_space=pltpu.SMEM)


def hbm():
    return pl.BlockSpec(memory_space=pl.ANY)


def normalise(values):
    average = jnp.mean(values, axis=-1, keepdims=True)
    centred = values - average
    inverse = lax.rsqrt(jnp.mean(centred * centred, axis=-1, keepdims=True) + EPS)
    return centred * inverse, inverse


def norm_back(grad, normal, inverse, gain):
    scaled_grad = grad * gain
    first_mean = jnp.mean(scaled_grad, axis=-1, keepdims=True)
    second_mean = jnp.mean(scaled_grad * normal, axis=-1, keepdims=True)
    return inverse * (scaled_grad - first_mean - normal * second_mean)


def shifted(window, by):
    return pltpu.roll(window, by % window.shape[0], 0)


def iota(shape, axis):
    return lax.broadcasted_iota(jnp.int32, shape, axis)


def times(index, size):
    return pl.ds(pl.multiple_of(index * size, size), size)


def position():
    index, batch = lax.axis_index("seq"), lax.axis_index("batch")
    return index // 2, index % 2, batch // 2, batch % 2


def at(z, core, y, x):
    return (z * 2 + core, y * 2 + x)


def remote(src, dst, send, recv, device):
    return pltpu.make_async_remote_copy(
        src_ref=src, dst_ref=dst, send_sem=send, recv_sem=recv, device_id=device, device_id_type=MESH
    )


def greet(others):
    barrier = pltpu.get_barrier_semaphore()
    for other in others:
        pl.semaphore_signal(barrier, inc=1, device_id=other, device_id_type=MESH)
    pl.semaphore_wait(barrier, len(others))


def whole_line():
    z, core, y, x = position()
    line = [at(lax.rem(z + step, 4), (core + turn) % 2, y, x) for turn in (0, 1) for step in (0, 1, 2, 3)]
    return line[1:]


def greet_all():
    z, core, y, x = position()
    greet(whole_line() + [at(z, core, 1 - y, x), at(z, core, y, 1 - x)])


def roles():
    z = lax.axis_index("seq") // 2
    half = z // 2
    near = jnp.where(half == 0, z, 3 - z)
    partner_z = jnp.where(half == 0, 1 - z, 5 - z)
    return half, near, partner_z, 2 - half


def z_of(half, place):
    return jnp.where(half == 0, place, 3 - place)


def long_source(seq, pair):
    near = 1 if pair % 3 == 2 else 0
    z = near if seq == 0 else 3 - near
    return z * 2 + pair // 3, 0 if near else pair % 3


def short_source(seq, pair):
    return (1 if seq == 0 else 2) * 2 + pair // 3, pair % 3


class Copies:
    def __init__(self, sems):
        self.sems, self.count, self.open = sems, 0, []

    def start(self, src, dst):
        copy = pltpu.make_async_copy(src, dst, self.sems.at[self.count])
        self.count += 1
        copy.start()
        self.open.append(copy)
        return copy

    def finish(self):
        for copy in self.open:
            copy.wait()
        self.open = []


class RowGather:
    def __init__(self, x_ref, o_ref, own_sem, send, recv, sib_send, sib_recv, inner_only):
        self.x_ref, self.o_ref, self.inner_only = x_ref, o_ref, inner_only
        self.own_sem, self.send, self.recv, self.sib_send, self.sib_recv = own_sem, send, recv, sib_send, sib_recv
        self.rows = x_ref.shape[1]
        self.z, self.core, self.y, self.x = position()
        self.half, self.near, self.partner_z, far_z = roles()
        self.sibling = at(self.z, 1 - self.core, self.y, self.x)
        self.partner = at(self.partner_z, self.core, self.y, self.x)
        place = self.block(self.z, self.core)
        mine, other = self.x_ref.at[self.half], self.x_ref.at[1 - self.half]
        self.to_partner = remote(mine, place, send.at[0], recv.at[self.near], self.partner)
        self.to_far = remote(other, place, send.at[1], recv.at[3 - self.near], at(far_z, self.core, self.y, self.x))
        self.to_sibling = remote(mine, place, sib_send.at[0], sib_recv.at[self.near], self.sibling)
        self.own = pltpu.make_async_copy(mine, place, own_sem)

    def block(self, z, core):
        return self.o_ref.at[times(z * 2 + core, self.rows)]

    def at_inner(self, act):
        if self.inner_only:
            pl.when(self.near == 1)(act)
        else:
            act()

    def start(self):
        if self.inner_only:
            pl.when(self.near == 0)(self.to_partner.start)
        else:
            self.to_partner.start()
        pl.when(self.near == 1)(self.to_far.start)

        def inside():
            self.to_sibling.start()
            self.own.start()

        self.at_inner(inside)

    def start_far(self):
        @pl.when(self.near == 0)
        def _():
            self.to_partner.wait_send()
            self.to_far.start()

    def moves(self, slot):
        place = (1 - self.near, 2, 3)[slot]
        block = self.block(z_of(self.half, place), self.core)
        arrival = remote(block, block, self.send.at[0], self.recv.at[place], self.partner)
        onward = remote(block, block, self.send.at[1 + slot], self.recv.at[place], self.partner)
        across = remote(block, block, self.sib_send.at[1 + slot], self.sib_recv.at[place], self.sibling)
        return arrival, onward, across

    def step(self, slot):
        arrival, onward, across = self.moves(slot)

        def inside():
            arrival.wait_recv()
            if slot and not self.inner_only:
                pl.when(self.near == 1)(onward.start)
            across.start()

        self.at_inner(inside)

    def whole(self, place):
        where = (self.near, 1 - self.near, 2, 3)[place]
        block = self.block(z_of(self.half, where), 1 - self.core)

        def inside():
            remote(block, block, self.sib_send.at[0], self.sib_recv.at[where], self.sibling).wait_recv()
            if place == 0:
                self.own.wait()

        self.at_inner(inside)

    def chip_rows(self, place):
        return z_of(self.half, (self.near, 1 - self.near, 2, 3)[place])

    def finish(self):
        if not self.inner_only:
            pl.when(self.near == 1)(self.to_partner.wait_send)
        self.to_far.wait_send()

        def inside():
            self.to_sibling.wait_send()
            for slot in range(3):
                _, onward, across = self.moves(slot)
                across.wait_send()
                if slot and not self.inner_only:
                    pl.when(self.near == 1)(onward.wait_send)

        self.at_inner(inside)


class ShardGather:
    def __init__(self, shard, full, own_sem, send, recv, halves=False):
        self.shard, self.full, self.own_sem, self.send_sem, self.recv_sem = shard, full, own_sem, send, recv
        self.z, self.core, self.y, self.x = position()
        self.halves = halves
        self.sent = []

    def go(self, src, dst, slot, device):
        copy = remote(src, dst, self.send_sem.at[slot], self.recv_sem.at[slot], device)
        copy.start()
        self.sent.append(copy)

    def arrived(self, dst, slot):
        remote(dst, dst, self.send_sem.at[0], self.recv_sem.at[slot], at(self.z, self.core, self.y, self.x)).wait_recv()

    def start(self):
        z, core, y, x = self.z, self.core, self.y, self.x
        mine = self.full.at[z, core, y, x]
        for step in (1, 2, 3):
            target = lax.rem(z + step, 4)
            self.go(self.shard, mine, step, at(target, core, y, x))
        self.own = pltpu.make_async_copy(self.shard, mine, self.own_sem)
        self.own.start()

    def part(self, core, zs, ys, xs, reader):
        ref = self.full.at[zs, core, ys, xs]
        return self.full.at[zs, core, ys, xs, reader] if self.halves else ref

    def across(self, zs, ys, xs, slot):
        ref = self.part(self.core, zs, ys, xs, 1 - self.core)
        self.go(ref, ref, slot, at(self.z, 1 - self.core, self.y, self.x))

    def over(self):
        z, core, y, x = self.z, self.core, self.y, self.x
        for step in (1, 2, 3):
            self.arrived(self.full.at[lax.rem(z + 4 - step, 4), core, y, x], step)
        self.own.wait()
        first, second = pl.ds(0, 2), pl.ds(2, 2)
        ref = self.full.at[first, core, y, x]
        self.go(ref, ref, 4, at(z, core, y, 1 - x))
        ref = self.full.at[second, core, y, x]
        self.go(ref, ref, 5, at(z, core, 1 - y, x))
        self.across(pl.ds(0, 4), y, x, 8)

    def turn(self):
        z, core, y, x = self.z, self.core, self.y, self.x
        first, second = pl.ds(0, 2), pl.ds(2, 2)
        self.arrived(self.full.at[first, core, y, 1 - x], 4)
        ref = self.full.at[first, core, y]
        self.go(ref, ref, 6, at(z, core, 1 - y, x))
        self.across(first, y, 1 - x, 9)
        self.arrived(self.full.at[second, core, 1 - y, x], 5)
        ref = self.full.at[second, core, :, x]
        self.go(ref, ref, 7, at(z, core, y, 1 - x))
        self.across(second, 1 - y, x, 10)

    def last(self):
        core, y, x = self.core, self.y, self.x
        first, second = pl.ds(0, 2), pl.ds(2, 2)
        self.arrived(self.full.at[first, core, 1 - y], 6)
        self.across(first, 1 - y, pl.ds(0, 2), 11)
        self.arrived(self.full.at[second, core, :, 1 - x], 7)
        self.across(second, pl.ds(0, 2), 1 - x, 12)

    def finish(self):
        y, x, core, other = self.y, self.x, self.core, 1 - self.core
        first, second, both = pl.ds(0, 2), pl.ds(2, 2), pl.ds(0, 2)
        parts = (
            (pl.ds(0, 4), y, x), (first, y, 1 - x), (second, 1 - y, x), (first, 1 - y, both), (second, both, 1 - x),
        )
        for slot, (zs, ys, xs) in enumerate(parts):
            self.arrived(self.part(other, zs, ys, xs, core), 8 + slot)

    def sends_done(self):
        for copy in self.sent:
            copy.wait_send()


def add_into(total, part):
    total[...] = (total[...].astype(F32) + part[...].astype(F32)).astype(total.dtype)


class CoreSum:
    def __init__(self, grad, sib, out, send, recv, save, hop=None):
        self.grad, self.sib, self.out, self.save = grad, sib, out, save
        self.z, self.core, self.y, self.x = position()
        z, core, y, x = position()
        self.copy = remote(grad.at[:, 1 - core], sib, send.at[0], recv.at[0], at(z, 1 - core, y, x))
        self.hop = hop
        first, second = pl.ds(0, 2), pl.ds(2, 2)
        if hop is not None:
            self.hops = (
                remote(sib.at[first, :, 1 - x], hop.at[0], send.at[1], recv.at[1], at(z, core, y, 1 - x)),
                remote(sib.at[second, 1 - y], hop.at[1], send.at[2], recv.at[2], at(z, core, 1 - y, x)),
            )

    def start(self):
        self.copy.start()

    def keep(self, *moves):
        self.kept = [pltpu.make_async_copy(src, dst, self.save.at[i]) for i, (src, dst) in enumerate(moves)]
        for copy in self.kept:
            copy.start()

    def add(self):
        self.copy.wait_recv()

        @pl.loop(0, 4)
        def _(zz):
            for ys in range(2):
                for xs in range(2):
                    add_into(self.sib.at[zz, ys, xs], self.grad.at[zz, self.core, ys, xs])

        if self.hop is None:
            self.keep((self.sib, self.out))
        else:
            for copy in self.hops:
                copy.start()

    def add_hop(self):
        x, y = self.x, self.y
        self.hops[0].wait_recv()
        for zz in range(2):
            for ys in range(2):
                add_into(self.sib.at[zz, ys, x], self.hop.at[0, zz, ys])
        self.hops[1].wait_recv()
        for zz in range(2):
            for xs in range(2):
                add_into(self.sib.at[2 + zz, y, xs], self.hop.at[1, zz, xs])
        self.keep(
            (self.sib.at[pl.ds(0, 2), :, x], self.out.at[0]),
            (self.sib.at[pl.ds(2, 2), y], self.out.at[1]),
        )

    def finish(self):
        self.copy.wait_send()
        for copy in self.kept:
            copy.wait()
        if self.hop is not None:
            for copy in self.hops:
                copy.wait_send()


class ShardSum:
    def __init__(self, grad, out, bufs, own_sem, send, recv, begun=False):
        self.grad, self.out, self.begun = grad, out, begun
        self.near_x, self.near_y, self.two, self.line = bufs[:4]
        self.one = None if begun else bufs[4]
        self.own_sem, self.send_sem, self.recv_sem = own_sem, send, recv
        self.z, self.core, self.y, self.x = position()
        self.sent = []
        first, second = pl.ds(0, 2), pl.ds(2, 2)
        self.loads = (
            pltpu.make_async_copy(grad.at[0] if begun else grad.at[first, :, self.x], self.near_x, own_sem.at[0]),
            pltpu.make_async_copy(grad.at[1] if begun else grad.at[second, self.y], self.near_y, own_sem.at[1]),
        )

    def copy(self, src, dst, slot, device):
        return remote(src, dst, self.send_sem.at[slot], self.recv_sem.at[slot], device)

    def go(self, src, dst, slot, device):
        copy = self.copy(src, dst, slot, device)
        copy.start()
        self.sent.append(copy)

    def arrived(self, dst, slot):
        remote(dst, dst, self.send_sem.at[0], self.recv_sem.at[slot], at(self.z, self.core, self.y, self.x)).wait_recv()

    def moves(self):
        z, core, y, x = self.z, self.core, self.y, self.x
        first, second = pl.ds(0, 2), pl.ds(2, 2)
        return ([] if self.begun else [
            self.copy(self.grad.at[first, :, 1 - x], self.one.at[0], 2, at(z, core, y, 1 - x)),
            self.copy(self.grad.at[second, 1 - y], self.one.at[1], 3, at(z, core, 1 - y, x)),
        ]) + [
            self.copy(self.near_x.at[:, 1 - y], self.two.at[0], 4, at(z, core, 1 - y, x)),
            self.copy(self.near_y.at[:, 1 - x], self.two.at[1], 5, at(z, core, y, 1 - x)),
        ]

    def to_line(self, step):
        z, core, y, x = self.z, self.core, self.y, self.x
        target = lax.rem(z + step, 4)
        device = at(target, core, y, x)
        low = self.copy(self.near_x.at[lax.rem(target, 2), y], self.line.at[step - 1], 5 + step, device)
        high = self.copy(self.near_y.at[lax.rem(target, 2), x], self.line.at[step - 1], 5 + step, device)
        return target, low, high

    def start(self):
        for copy in self.moves()[:-2]:
            copy.start()
        for copy in self.loads:
            copy.start()

    def turn(self):
        moves = self.moves()
        for side, near in enumerate((self.near_x, self.near_y)):
            self.loads[side].wait()
            if not self.begun:
                self.arrived(self.one.at[side], 2 + side)
                for zz in range(2):
                    for other in range(2):
                        add_into(near.at[zz, other], self.one.at[side, zz, other])
            moves[side - 2].start()

    def last(self):
        y, x = self.y, self.x
        self.arrived(self.two.at[0], 4)
        for zz in range(2):
            add_into(self.near_x.at[zz, y], self.two.at[0, zz])
        self.arrived(self.two.at[1], 5)
        for zz in range(2):
            add_into(self.near_y.at[zz, x], self.two.at[1, zz])
        for step in (1, 2, 3):
            target, low, high = self.to_line(step)
            pl.when(target < 2)(low.start)
            pl.when(target >= 2)(high.start)

    def finish(self):
        z, y, x = self.z, self.y, self.x
        low = self.near_x[lax.rem(z, 2), y].astype(F32)
        high = self.near_y[lax.rem(z, 2), x].astype(F32)
        total = jnp.where(z < 2, low, high)
        for step in (1, 2, 3):
            self.arrived(self.line.at[step - 1], 5 + step)
            total = total + self.line[step - 1].astype(F32)
        self.out[...] = total
        for copy in self.moves():
            copy.wait_send()
        for step in (1, 2, 3):
            target, low, high = self.to_line(step)
            pl.when(target < 2)(low.wait_send)
            pl.when(target >= 2)(high.wait_send)

    @staticmethod
    def buffers(grad, begun=False):
        tail, kind = grad.shape[3:], grad.dtype
        shapes = [(2, 2), (2, 2), (2, 2), (3,)] + ([] if begun else [(2, 2, 2)])
        return [pltpu.VMEM(shape + tail, kind) for shape in shapes]


class GroupSum:
    def __init__(self, bufs, send, recv):
        self.tot, self.one, self.two, self.line = bufs
        self.send_sem, self.recv_sem = send, recv
        self.z, self.core, self.y, self.x = position()
        self.sent = []

    copy = ShardSum.copy
    go = ShardSum.go
    arrived = ShardSum.arrived

    def start(self, total, columns):
        z, core, y, x = self.z, self.core, self.y, self.x
        rows = self.tot.shape[4]

        @pl.loop(0, 4)
        def _(zz):
            for cc in range(2):
                for yy in range(2):
                    for xx in range(2):
                        first = pl.multiple_of(zz * 8 * rows, 8) + ((cc * 2 + yy) * 2 + xx) * rows
                        part = total[pl.ds(pl.multiple_of(first, 8), rows), columns]
                        self.tot[zz, cc, yy, xx] = part.astype(BF16)

        self.go(self.tot.at[pl.ds(0, 2), :, :, 1 - x], self.one.at[0], 0, at(z, core, y, 1 - x))
        self.go(self.tot.at[pl.ds(2, 2), :, 1 - y], self.one.at[1], 1, at(z, core, 1 - y, x))

    def turn(self):
        z, core, y, x = self.z, self.core, self.y, self.x
        self.arrived(self.one.at[0], 0)

        @pl.loop(0, 2)
        def _(zz):
            for cc in range(2):
                for ys in range(2):
                    add_into(self.tot.at[zz, cc, ys, x], self.one.at[0, zz, cc, ys])

        self.go(self.tot.at[pl.ds(0, 2), :, 1 - y, x], self.two.at[0], 2, at(z, core, 1 - y, x))
        self.arrived(self.one.at[1], 1)

        @pl.loop(0, 2)
        def _(zz):
            for cc in range(2):
                for xs in range(2):
                    add_into(self.tot.at[2 + zz, cc, y, xs], self.one.at[1, zz, cc, xs])

        self.go(self.tot.at[pl.ds(2, 2), :, y, 1 - x], self.two.at[1], 3, at(z, core, y, 1 - x))

    def last(self):
        z, core, y, x = self.z, self.core, self.y, self.x
        for side in (0, 1):
            self.arrived(self.two.at[side], 2 + side)

            @pl.loop(0, 2)
            def _(zz, side=side):
                for cc in range(2):
                    add_into(self.tot.at[2 * side + zz, cc, y, x], self.two.at[side, zz, cc])

        mine = z * 2 + core
        for step in range(1, 8):
            target = lax.rem(mine + step, 8)
            tz, tc = target // 2, target % 2
            self.go(self.tot.at[tz, tc, y, x], self.line.at[step - 1], 3 + step, at(tz, tc, y, x))

    def finish(self):
        for step in range(1, 8):
            self.arrived(self.line.at[step - 1], 3 + step)
        for copy in self.sent:
            copy.wait_send()

    def term(self, source):
        z, core, y, x = self.z, self.core, self.y, self.x
        back = lax.rem(z * 2 + core - source + 8 + 7, 8)
        own = self.tot[z, core, y, x].astype(F32)
        return jnp.where(back == 7, own, self.line[jnp.minimum(back, 6)].astype(F32))

    @staticmethod
    def buffers(rows, columns):
        return [
            pltpu.VMEM((4, 2, 2, 2, rows, columns), BF16),
            pltpu.VMEM((2, 2, 2, 2, rows, columns), BF16),
            pltpu.VMEM((2, 2, 2, rows, columns), BF16),
            pltpu.VMEM((7, rows, columns), BF16),
        ]


def join_groups(first, second, out):
    width = out.shape[1] // 3
    for side in range(2):
        early = None
        for z in range(4):
            term = first.term(z * 2 + side)
            early = term if early is None else early + term
        outer = second.term(side) + second.term(6 + side)
        inner = second.term(2 + side) + second.term(4 + side)
        pairs = (early[:, :TRIPLE], early[:, TRIPLE:] + outer, inner)
        for j, pair in enumerate(pairs):
            for kind in range(3):
                target = kind * width + (3 * side + j) * LANES
                out[:, target : target + LANES] = pair[:, kind * LANES : (kind + 1) * LANES]


class SmallSum:
    def __init__(self, bufs, out, send, recv):
        self.norms, self.swap, self.acc, self.got, self.line = bufs
        self.out, self.send_sem, self.recv_sem = out, send, recv
        self.z, self.core, self.y, self.x = position()
        self.sent = []
        self.cut = self.norms.shape[2]

    copy = ShardSum.copy
    go = ShardSum.go
    arrived = ShardSum.arrived

    def start(self, kernel_grad, norm_grad):
        z, core, y, x = self.z, self.core, self.y, self.x
        cut = self.cut
        self.norms[0] = norm_grad[:, :cut]
        self.norms[1] = norm_grad[:, cut:]
        self.acc[0, :, : kernel_grad.shape[1]] = kernel_grad
        self.go(self.norms.at[1 - core], self.swap, 0, at(z, 1 - core, y, x))

    def over(self):
        z, core, y, x = self.z, self.core, self.y, self.x
        self.arrived(self.swap, 0)
        self.acc[0, :, self.acc.shape[2] - self.cut :] = self.norms[core] + self.swap[...]
        self.go(self.acc.at[0], self.got.at[0], 1, at(z, core, y, 1 - x))

    def turn(self):
        z, core, y, x = self.z, self.core, self.y, self.x
        self.arrived(self.got.at[0], 1)
        self.acc[1] = self.acc[0] + self.got[0]
        self.go(self.acc.at[1], self.got.at[1], 2, at(z, core, 1 - y, x))

    def last(self):
        z, core, y, x = self.z, self.core, self.y, self.x
        self.arrived(self.got.at[1], 2)
        self.acc[2] = self.acc[1] + self.got[1]
        for step in (1, 2, 3):
            self.go(self.acc.at[2], self.line.at[step - 1], 2 + step, at(lax.rem(z + step, 4), core, y, x))

    def swap_back(self):
        z, core, y, x = self.z, self.core, self.y, self.x
        for step in (1, 2, 3):
            self.arrived(self.line.at[step - 1], 2 + step)
        total = None
        for source in range(4):
            back = lax.rem(z - source + 4, 4)
            term = jnp.where(back == 0, self.acc[2], self.line[jnp.maximum(back - 1, 0)])
            total = term if total is None else total + term
        self.out[core] = total
        self.go(self.out.at[core], self.out.at[core], 6, at(z, 1 - core, y, x))

    def finish(self):
        self.arrived(self.out.at[1 - self.core], 6)
        for copy in self.sent:
            copy.wait_send()

    @staticmethod
    def buffers(columns, norm_columns):
        wide = columns + norm_columns
        return [
            pltpu.VMEM((2, 8, norm_columns), F32),
            pltpu.VMEM((8, norm_columns), F32),
            pltpu.VMEM((3, 8, wide), F32),
            pltpu.VMEM((2, 8, wide), F32),
            pltpu.VMEM((3, 8, wide), F32),
        ]


def causal_mask():
    return iota((TILE, TILE), 0) <= iota((TILE, TILE), 1)


def place_small(smalls, kernel_out, norm_out, core, part, cut):
    wide, width = kernel_out.shape[1], norm_out.shape[1]
    column = iota((LANES, wide), 1)
    block, lane = column // LANES, column % LANES
    source = (block % 3) * width + (core * 3 + block // 3) * LANES + lane - iota((LANES, wide), 0)
    norm_source = iota((LANES, width), 1) - iota((LANES, width), 0)
    kernel_out[...] = jnp.zeros_like(kernel_out)
    norm_out[...] = jnp.zeros_like(norm_out)

    @pl.loop(0, smalls.shape[0])
    def _(device):
        low = smalls[device].astype(BF16)
        kernel_out[...] += dot_nn(low, jnp.where(source == device * part, 1.0, 0.0).astype(BF16))
        norm_out[...] += dot_nn(low, jnp.where(norm_source == device * cut, 1.0, 0.0).astype(BF16))

    norm_out[0:4] = norm_out[3:7]


def attend(query_ref, key_ref, value_t, lse, out_t, head, block):
    rows, past = slice(block * TILE, (block + 1) * TILE), slice(0, block * TILE)
    query = query_ref[head, rows]
    diagonal = jnp.where(causal_mask(), dot_nt(key_ref[head, rows], query), NEG_FILL)
    top = jnp.max(diagonal, axis=0, keepdims=True)
    if block:
        before = dot_nt(key_ref[head, past], query)
        top = jnp.maximum(top, jnp.max(before, axis=0, keepdims=True))
        exp_before = jnp.exp(before - top)
    exp_diagonal = jnp.exp(diagonal - top)
    norm = jnp.sum(exp_diagonal, axis=0, keepdims=True)
    if block:
        norm = norm + jnp.sum(exp_before, axis=0, keepdims=True)
    lse[head, :, rows] = top + jnp.log(norm)
    inverse = 1.0 / norm
    result = dot_nn(value_t[head, :, rows], (exp_diagonal * inverse).astype(BF16))
    if block:
        result = result + dot_nn(value_t[head, :, past], (exp_before * inverse).astype(BF16))
    out_t[head, :, rows] = result


def convolve(proj, taps, slot, local, start, length, query_ref, key_ref, value_ref, key_t, value_t):
    window = proj[slot, pl.ds(pl.multiple_of(start, PAD), TILE + PAD)].astype(F32)
    columns = times(local, TRIPLE)
    mixed = (
        taps[0:1, columns] * window[PAD:]
        + taps[1:2, columns] * shifted(window, 1)[PAD:]
        + taps[2:3, columns] * shifted(window, 2)[PAD:]
    ).astype(BF16).astype(F32)
    query, key, value = mixed[:, 0:LANES] * (HEAD_DIM**-0.5), mixed[:, LANES : 2 * LANES], mixed[:, 2 * LANES :]
    rows = pl.ds(pl.multiple_of(start, TILE), TILE)
    lanes = iota((TILE, LANES), 1)
    low_half = lanes < HEAD_DIM
    bias = jnp.where(start + iota((TILE, LANES), 0) < length, 0.0, NEG_FILL)
    at_zero, at_half = lanes == 0, lanes == HEAD_DIM
    query_ref[2 * slot, rows] = jnp.where(low_half, query, jnp.where(at_half, 1.0, 0.0)).astype(BF16)
    query_ref[2 * slot + 1, rows] = jnp.where(low_half, jnp.where(at_zero, 1.0, 0.0), query).astype(BF16)
    key_ref[2 * slot, rows] = jnp.where(low_half, key, jnp.where(at_half, bias, 0.0)).astype(BF16)
    key_ref[2 * slot + 1, rows] = jnp.where(low_half, jnp.where(at_zero, bias, 0.0), key).astype(BF16)
    value_ref[slot, rows] = value.astype(BF16)
    turned_key, turned_value = key.T.astype(BF16), value.T.astype(BF16)
    for head in range(2):
        part = slice(head * HEAD_DIM, (head + 1) * HEAD_DIM)
        key_t[2 * slot + head, :, rows] = turned_key[part]
        value_t[2 * slot + head, :, rows] = turned_value[part]


def first_kernel(
    lens, xs_ref, xl_ref, qkv_ref, conv_ref, norm_ref, out_s, up_s, down_s,
    att, full_out, full_up, full_down, xs_o, xl_o, wq_o, taps_o, norms_o,
    ql_o, kl_o, vl_o, ktl_o, lsel_o, pl_o, ol_o, qs_o, ks_o, vs_o, kts_o, lses_o, ps_o, os_o,
    xs, xl, small, smalls, shard, wq_parts, wq, taps, norms,
    ql, kl, vl, ktl, lsel, proj_l, ol, qs, ks, vs, kts, lses, proj_s, os,
    vtl, vts, otl, ots,
    own_sem, send, recv, sib_send, sib_recv, shard_own, shard_send, shard_recv,
    att_send_l, att_recv_l, att_send_s, att_recv_s, att_own_l, att_own_s, save_sem,
):
    z, core, y, x = position()
    half, near, _, _ = roles()
    index = z * 2 + core
    pairs_long = 2 - near
    own_short, own_long = xs_ref.shape[1], xl_ref.shape[1]
    long_rows, short_rows = xl.shape[0], xs.shape[0]
    part, cut = conv_ref.shape[1], norm_ref.shape[1]
    length_short = jnp.where(half == 0, lens[0, 0], lens[0, 1])
    length_long = jnp.where(half == 0, lens[1, 0], lens[1, 1])

    small[...] = jnp.zeros_like(small)
    small[0:3, 0:part] = conv_ref[...].astype(F32)
    small[3:7, 0:cut] = norm_ref[...].astype(F32)
    width = wq.shape[0]
    for side in range(2):
        for j in range(3):
            for kind in range(3):
                source = kind * width + (3 * side + j) * LANES
                target = (3 * j + kind) * LANES
                shard[side, :, target : target + LANES] = qkv_ref[:, source : source + LANES]
    greet_all()
    rows_short = RowGather(
        xs_ref, xs, own_sem.at[0], send.at[0], recv.at[0], sib_send.at[0], sib_recv.at[0], True
    )
    rows_long = RowGather(
        xl_ref, xl, own_sem.at[1], send.at[1], recv.at[1], sib_send.at[1], sib_recv.at[1], False
    )
    weights = [
        ShardGather(a, f, shard_own.at[i], shard_send.at[i], shard_recv.at[i], halves=i == 1)
        for i, (a, f) in enumerate(
            ((small, smalls), (shard, wq_parts), (out_s, full_out), (up_s, full_up), (down_s, full_down))
        )
    ]
    small_w, qkv_w, out_w, up_w, down_w = weights

    def place():
        place_small(smalls.reshape(32, 8, LANES), taps, norms, core, part, cut)

    def join_weights():
        pieces = wq_parts.shape[5]
        for zz in range(4):
            for cc in range(2):
                for yy in range(2):
                    first = ((zz * 2 + cc) * 2 + yy) * 2 * pieces
                    both = jnp.concatenate([wq_parts[zz, cc, yy, xx, core].astype(F32) for xx in range(2)], axis=0)
                    wq[first : first + 2 * pieces] = both.astype(BF16)

    def project(x_ref, proj, start, size, slots, first_pair):
        normal, _ = normalise(x_ref[pl.ds(pl.multiple_of(start, size), size)].astype(F32))
        low = (normal * norms[0:1] + norms[1:2]).astype(BF16)

        @pl.loop(0, slots)
        def _(slot):
            result = dot_nn(low, wq[:, times(slot + first_pair, TRIPLE)])
            proj[slot, pl.ds(pl.multiple_of(PAD + start, PAD), size)] = result.astype(BF16)

    def project_long(place):
        @pl.loop(0, 2)
        def _(side):
            project(xl, proj_l, rows_long.chip_rows(place) * 2 * own_long + side * TILE, TILE, pairs_long, 2 * near)

    def project_short(place):
        @pl.when(near == 1)
        def _():
            project(xs, proj_s, rows_short.chip_rows(place) * 2 * own_short, TILE, 3, 0)

    def conv_short():
        @pl.when(near == 1)
        def _():
            @pl.loop(0, 3)
            def _(slot):
                @pl.loop(0, short_rows // TILE)
                def _(step):
                    convolve(proj_s, taps, slot, slot, step * TILE, length_short, qs, ks, vs, kts, vts)

    def conv_long():
        @pl.loop(0, pairs_long)
        def _(slot):
            @pl.loop(0, long_rows // TILE)
            def _(step):
                convolve(proj_l, taps, slot, slot + 2 * near, step * TILE, length_long, ql, kl, vl, ktl, vtl)

    saves = Copies(save_sem)

    def save(*moves):
        for source, target in moves:
            saves.start(source, target)

    def save_long():
        save((xl, xl_o), (wq, wq_o), (taps, taps_o), (norms, norms_o))
        save((ql, ql_o), (kl, kl_o), (vl, vl_o), (ktl, ktl_o), (proj_l, pl_o))

    def save_short():
        save((xs, xs_o), (qs, qs_o), (ks, ks_o), (vs, vs_o))
        save((kts, kts_o), (proj_s, ps_o), (lses, lses_o), (os, os_o))

    def save_last():
        save((lsel, lsel_o), (ol, ol_o))

    def to_owner(o_ref, slot, first, rows, owner, row_in_owner, pair, send_sem, recv_sem, own_sem):
        source = o_ref.at[slot, pl.ds(first, rows)]
        target = att.at[
            pl.ds(pl.multiple_of(row_in_owner, LANES), rows), times(pair, LANES)
        ]
        far = remote(source, target, send_sem, recv_sem, (owner, y * 2 + x))
        close = pltpu.make_async_copy(source, target, own_sem)
        return far, close

    def short_moves(slot, owner):
        return to_owner(
            os, slot, owner * own_short, own_short, owner, 2 * own_long + half * own_short, 3 * core + slot,
            att_send_s.at[slot, owner], att_recv_s.at[half, 3 * core + slot], att_own_s.at[slot],
        )

    def long_moves(slot, owner):
        pair = 3 * core + slot + 2 * near
        return to_owner(
            ol, slot, owner * own_long, own_long, owner, half * own_long, pair,
            att_send_l.at[slot, owner], att_recv_l.at[half, pair], att_own_l.at[slot],
        )

    def send_block(o_ref, o_t, slot, block, moves, owners):
        rows = slice(block * TILE, (block + 1) * TILE)
        both = jnp.concatenate([o_t[2 * slot, :, rows], o_t[2 * slot + 1, :, rows]], axis=0)
        o_ref[slot, rows] = both.T.astype(BF16)
        for owner in owners:
            far, close = moves(slot, owner)
            pl.when(index != owner)(far.start)
            pl.when(index == owner)(close.start)

    def attend_short(block):
        @pl.when(near == 1)
        def _():
            @pl.loop(0, 6)
            def _(head):
                attend(qs, ks, vts, lses, ots, head, block)

    def send_short(block):
        @pl.when(near == 1)
        def _():
            @pl.loop(0, 3)
            def _(slot):
                send_block(os, ots, slot, block, short_moves, (2 * block, 2 * block + 1))

    def attend_long(block):
        @pl.loop(0, 2 * pairs_long)
        def _(head):
            attend(ql, kl, vtl, lsel, otl, head, block)

    def send_long(block):
        @pl.loop(0, pairs_long)
        def _(slot):
            send_block(ol, otl, slot, block, long_moves, (block,))

    zeros = jnp.zeros((PAD, TRIPLE), BF16)
    for slot in range(2):
        proj_l[slot, 0:PAD] = zeros
    for slot in range(3):
        proj_s[slot, 0:PAD] = zeros
    small_w.start()
    qkv_w.start()
    rows_long.start()
    rows_long.start_far()
    rows_short.start()
    small_w.over()
    small_w.turn()
    small_w.last()
    small_w.finish()
    place()
    qkv_w.over()
    rows_long.step(0)
    qkv_w.turn()
    rows_short.start_far()
    up_w.start()
    out_w.start()
    rows_long.step(1)
    qkv_w.last()
    rows_long.step(2)
    down_w.start()
    qkv_w.finish()
    join_weights()
    rows_long.whole(0)
    project_long(0)
    rows_long.whole(1)
    project_long(1)
    rows_long.whole(2)
    project_long(2)
    rows_short.step(0)
    rows_short.step(1)
    rows_short.step(2)
    rows_short.whole(0)
    project_short(0)
    rows_short.whole(1)
    project_short(1)
    rows_short.whole(2)
    project_short(2)
    rows_short.whole(3)
    project_short(3)
    rows_long.whole(3)
    project_long(3)
    up_w.over()
    out_w.over()
    conv_short()
    attend_short(0)
    send_short(0)
    attend_short(2)
    send_short(2)
    attend_short(1)
    send_short(1)
    attend_short(3)
    send_short(3)
    save_short()
    conv_long()
    save_long()
    attend_long(0)
    send_long(0)
    up_w.turn()
    attend_long(4)
    send_long(4)
    out_w.turn()
    attend_long(1)
    send_long(1)
    attend_long(5)
    send_long(5)
    down_w.over()
    up_w.last()
    out_w.last()
    attend_long(2)
    send_long(2)
    attend_long(6)
    send_long(6)
    down_w.turn()
    attend_long(3)
    send_long(3)
    attend_long(7)
    send_long(7)
    save_last()
    down_w.last()
    out_w.finish()
    up_w.finish()
    down_w.finish()
    for one in weights:
        one.sends_done()

    def own_or_wait(source, moves, slot, arrival):
        @pl.when(index == source)
        def _():
            moves(slot, index)[1].wait()

        @pl.when(index != source)
        def _():
            arrival.wait_recv()

    me = (index, y * 2 + x)
    for seq in range(2):
        for pair in range(6):
            columns = pl.ds(pair * LANES, LANES)
            block = att.at[pl.ds(seq * own_long, own_long), columns]
            source, slot = long_source(seq, pair)
            own_or_wait(
                source, long_moves, slot,
                remote(block, block, att_send_l.at[0, 0], att_recv_l.at[seq, pair], me),
            )
            block = att.at[pl.ds(2 * own_long + seq * own_short, own_short), columns]
            source, slot = short_source(seq, pair)
            own_or_wait(
                source, short_moves, slot,
                remote(block, block, att_send_s.at[0, 0], att_recv_s.at[seq, pair], me),
            )

    def sends_done(moves, slot):
        for owner in range(8):
            far, _ = moves(slot, owner)
            pl.when(index != owner)(far.wait_send)

    sends_done(long_moves, 0)
    pl.when(near == 0)(lambda: sends_done(long_moves, 1))

    @pl.when(near == 1)
    def _():
        for slot in range(3):
            sends_done(short_moves, slot)

    rows_long.finish()
    rows_short.finish()
    saves.finish()


def first_part(lengths, x_short, x_long, w_qkv, conv_kernel, norm_params, w_out, w_up, w_down, count):
    width = x_short.shape[2]
    short, long = count * x_short.shape[1], count * x_long.shape[1]
    owned = x_short.shape[1] + x_long.shape[1]
    wide = w_qkv.shape[1] // 2
    rows = w_qkv.shape[0]
    out = jax.ShapeDtypeStruct

    def saved(pairs, total):
        return [
            ((2 * pairs, total, LANES), BF16),
            ((2 * pairs, total, LANES), BF16),
            ((pairs, total, LANES), BF16),
            ((2 * pairs, HEAD_DIM, total), BF16),
            ((2 * pairs, 1, total), F32),
            ((pairs, PAD + total, TRIPLE), BF16),
            ((pairs, total, LANES), BF16),
        ]

    kept = saved(2, long) + saved(3, short)
    basic = [((short, width), BF16), ((long, width), BF16)]
    consts = [((width, wide), BF16), ((8, wide), F32), ((8, width), F32)]
    full = [((4, 2, 2, 2) + w.shape, BF16) for w in (w_out, w_up, w_down)]
    outs = [((2 * owned, width), BF16)] + full + basic + consts + kept
    scratch = (
        basic
        + [((8, LANES), F32), ((4, 2, 2, 2, 8, LANES), F32), ((2, rows, wide), BF16)]
        + [((4, 2, 2, 2, 2, rows, wide), BF16)]
        + consts
        + kept
        + [((4, HEAD_DIM, long), BF16), ((6, HEAD_DIM, short), BF16)]
        + [((4, HEAD_DIM, long), F32), ((6, HEAD_DIM, short), F32)]
    )
    return pl.pallas_call(
        first_kernel,
        out_shape=tuple(out(*one) for one in outs),
        in_specs=[smem(), hbm(), hbm(), vmem(), vmem(), vmem(), hbm(), hbm(), hbm()],
        out_specs=tuple([hbm()] * len(outs)),
        scratch_shapes=[pltpu.VMEM(*one) for one in scratch]
        + [DMA((2,))] + [DMA((2, 4))] * 4
        + [DMA((5,)), DMA((5, 13)), DMA((5, 13))]
        + [DMA((2, 8)), DMA((2, 6)), DMA((3, 8)), DMA((2, 6)), DMA((2,)), DMA((3,))]
        + [DMA((24,))],
        compiler_params=params_of(collective_id=0, has_side_effects=True),
    )(lengths, x_short, x_long, w_qkv, conv_kernel, norm_params, w_out, w_up, w_down)


def second_kernel(
    xs_ref, xl_ref, att, cs_ref, cl_ref, np_ref, wo_ref, wu_ref, wd_ref,
    ys_ref, yl_ref, gmid, gnorm, gwo_o, gwu_o, gwd_o, gl_o, gs_o,
    wo, wu, wd, middle, normal_two, inverse_two, second, second_t, cot, y_acc, gsec, gml, hid, gup,
    gwo, gwu, gwd, sib_out, sib_up, sib_down,
    load_sem, save_sem, send_l, recv_l, send_s, recv_s, core_send, core_recv,
):
    z, core, y, x = position()
    half, near, _, _ = roles()
    index = z * 2 + core
    pairs_long = 2 - near
    loads = Copies(load_sem)
    got_out = loads.start(wo_ref, wo)
    got_up = loads.start(wu_ref, wu)
    got_down = loads.start(wd_ref, wd)
    greet_all()
    short, long = xs_ref.shape[1], xl_ref.shape[1]
    first_short = 2 * long
    for seq in range(2):
        rows = slice(seq * long, (seq + 1) * long)
        cot[rows] = cl_ref[seq]
        middle[rows] = xl_ref[seq].astype(F32)
        rows = slice(first_short + seq * short, first_short + (seq + 1) * short)
        cot[rows] = cs_ref[seq]
        middle[rows] = xs_ref[seq].astype(F32)
    gnorm[...] = jnp.zeros_like(gnorm)
    inner = 512

    def through(part, size):
        @pl.loop(0, size // TILE)
        def _(step):
            rows = pl.ds(pl.multiple_of(part + step * TILE, TILE), TILE)
            values = middle[rows] + dot_nn(att[rows], wo[...])
            normal, inverse = normalise(values)
            normal_two[rows] = normal
            inverse_two[rows] = inverse
            second[rows] = (normal * np_ref[2:3] + np_ref[3:4]).astype(BF16)
            y_acc[rows] = values
            gsec[rows] = jnp.zeros_like(values)

        all_rows = slice(part, part + size)
        second_t[:, all_rows] = second[all_rows].T
        if part == 0:
            got_up.wait()
            got_down.wait()

        @pl.loop(0, wu.shape[1] // inner)
        def _(step):
            columns = times(step, inner)
            upper = jnp.maximum(dot_nn(second[all_rows], wu[:, columns]), 0.0)
            hidden = (upper * upper).astype(BF16)
            grad_hidden = dot_nt(cot[all_rows], wd[columns])
            grad_upper = (2.0 * upper * grad_hidden).astype(BF16)
            hid[all_rows, columns] = hidden
            gup[all_rows, columns] = grad_upper
            y_acc[all_rows] += dot_nn(hidden, wd[columns])
            gsec[all_rows] += dot_nt(grad_upper, wu[:, columns])

        @pl.loop(0, size // TILE)
        def _(step):
            rows = pl.ds(pl.multiple_of(part + step * TILE, TILE), TILE)
            grad = gsec[rows]
            normal = normal_two[rows]
            gnorm[2:3] += jnp.sum(grad * normal, axis=0, keepdims=True)
            gnorm[3:4] += jnp.sum(grad, axis=0, keepdims=True)
            total = cot[rows].astype(F32) + norm_back(grad, normal, inverse_two[rows], np_ref[2:3])
            gmid[rows] = total
            gml[rows] = total.astype(BF16)
            second[rows] = dot_nt(gml[rows], wo[...]).astype(BF16)

    def moves(seq, pair, is_long):
        target, slot = (long_source if is_long else short_source)(seq, pair)
        rows = long if is_long else short
        out, send, recv = (gl_o, send_l, recv_l) if is_long else (gs_o, send_s, recv_s)
        first = seq * long if is_long else first_short + seq * short
        source = second.at[pl.ds(first, rows), pl.ds(pair * LANES, LANES)]
        place = out.at[slot, times(index, rows)]
        far = remote(source, place, send.at[seq, pair], recv.at[slot, index], (target, y * 2 + x))
        close = pltpu.make_async_copy(source, place, recv.at[slot, index])
        return target, far, close

    kinds = [(seq, pair, is_long) for is_long in (True, False) for pair in range(6) for seq in range(2)]

    def send_part(is_long):
        for kind in kinds:
            if kind[2] == is_long:
                target, far, close = moves(*kind)
                pl.when(index != target)(far.start)
                pl.when(index == target)(close.start)

    got_out.wait()
    through(0, first_short)
    send_part(True)
    through(first_short, 2 * short)
    send_part(False)

    sums = [
        CoreSum(grad, sib, total, core_send.at[i], core_recv.at[i], save_sem.at[i], hop)
        for i, (grad, sib, total, hop) in enumerate(
            ((gwu, sib_up, gwu_o, None), (gwd, sib_down, gwd_o, None), (gwo, sib_out, gwo_o, None))
        )
    ]

    def cut(value, grad):
        return value.reshape(grad.shape[:5] + value.shape[1:]).astype(BF16)

    @pl.loop(0, wu.shape[1] // inner)
    def _(step):
        columns = times(step, inner)
        gwu[:, :, :, :, :, columns] = cut(dot_nn(second_t[...], gup[:, columns]), gwu)

    sums[0].start()
    per = gwd.shape[4]
    slabs = gwd.shape[2] * gwd.shape[3]

    @pl.loop(0, gwd.shape[0])
    def _(zz):
        for cc in range(2):
            columns = times(zz * 2 + cc, slabs * per)
            value = dot_tn(hid[:, columns], cot[...])
            gwd[zz, cc] = value.reshape(gwd.shape[2:]).astype(BF16)

    sums[1].start()
    sums[0].add()
    gwo[...] = cut(dot_tn(att[...], gml[...]), gwo)
    sums[2].start()
    for seq in range(2):
        ys_ref[seq] = y_acc[first_short + seq * short : first_short + (seq + 1) * short].astype(BF16)
        yl_ref[seq] = y_acc[seq * long : (seq + 1) * long].astype(BF16)

    sums[1].add()
    sums[2].add()
    me = (index, y * 2 + x)

    def arrivals(out, recv, slot, rows):
        for source in range(8):
            block = out.at[slot, pl.ds(source * rows, rows)]

            @pl.when(index != source)
            def _(block=block, source=source):
                remote(block, block, send_l.at[0, 0], recv.at[slot, source], me).wait_recv()

    arrivals(gl_o, recv_l, 0, long)
    pl.when(near == 0)(lambda: arrivals(gl_o, recv_l, 1, long))

    @pl.when(near == 1)
    def _():
        for slot in range(3):
            arrivals(gs_o, recv_s, slot, short)

    for kind in kinds:
        target, far, close = moves(*kind)
        pl.when(index != target)(far.wait_send)
        pl.when(index == target)(close.wait)
    for one in sums:
        one.finish()


def second_part(x_short, x_long, att, cot_short, cot_long, norms, w_out, w_up, w_down, count):
    width = x_short.shape[2]
    rows = att.shape[0]
    short, long = count * x_short.shape[1], count * x_long.shape[1]
    hidden = w_up.shape[1]
    out = jax.ShapeDtypeStruct
    devices = 4 * count

    def shards(w):
        return (4, 2, 2, 2, w.shape[0] // devices, w.shape[1])

    def halves(w):
        return (4, 2, 2, w.shape[0] // devices, w.shape[1])

    return pl.pallas_call(
        second_kernel,
        out_shape=(
            out(x_short.shape, BF16),
            out(x_long.shape, BF16),
            out((rows, width), F32),
            out((8, width), F32),
            out(halves(w_out), BF16),
            out(halves(w_up), BF16),
            out(halves(w_down), BF16),
            out((2, long, LANES), BF16),
            out((3, short, LANES), BF16),
        ),
        in_specs=[vmem()] * 6 + [hbm()] * 3,
        out_specs=tuple([vmem()] * 4 + [hbm()] * 5),
        scratch_shapes=[
            pltpu.VMEM(w_out.shape, BF16),
            pltpu.VMEM(w_up.shape, BF16),
            pltpu.VMEM(w_down.shape, BF16),
            pltpu.VMEM((rows, width), F32),
            pltpu.VMEM((rows, width), F32),
            pltpu.VMEM((rows, 1), F32),
            pltpu.VMEM((rows, width), BF16),
            pltpu.VMEM((width, rows), BF16),
            pltpu.VMEM((rows, width), BF16),
            pltpu.VMEM((rows, width), F32),
            pltpu.VMEM((rows, width), F32),
            pltpu.VMEM((rows, width), BF16),
            pltpu.VMEM((rows, hidden), BF16),
            pltpu.VMEM((rows, hidden), BF16),
            *[pltpu.VMEM(shards(w), BF16) for w in (w_out, w_up, w_down)],
            *[pltpu.VMEM(halves(w), BF16) for w in (w_out, w_up, w_down)],
            DMA((3,)), DMA((3, 2)), DMA((2, 6)), DMA((2, 8)), DMA((2, 6)), DMA((3, 8)), DMA((3, 3)), DMA((3, 3)),
        ],
        compiler_params=params_of(collective_id=1, has_side_effects=True),
    )(x_short, x_long, att, cot_short, cot_long, norms, w_out, w_up, w_down)


class RowSum:
    def __init__(self, long_bufs, short_bufs, sems):
        self.mine, self.out, self.sib, self.got, self.fin = long_bufs
        self.mine_s, self.out_s, self.sib_s, self.fin_s = short_bufs
        (
            self.sib_send, self.sib_recv, self.send, self.recv, self.on_send, self.fin_recv,
            self.sib_send_s, self.sib_recv_s, self.send_s, self.fin_recv_s,
        ) = sems
        self.z, self.core, self.y, self.x = position()
        self.half, self.near, partner_z, far_z = roles()
        self.partner = at(partner_z, self.core, self.y, self.x)
        self.sibling = at(self.z, 1 - self.core, self.y, self.x)
        self.far = at(far_z, self.core, self.y, self.x)

    def across(self, zz):
        return remote(self.out.at[zz % 2], self.sib.at[zz], self.sib_send.at[zz], self.sib_recv.at[zz], self.sibling)

    def put(self, block, value):
        zz, parity = block // 2, block % 2

        @pl.when(self.core == parity)
        def _():
            self.mine[zz] = value

        @pl.when(self.core != parity)
        def _():
            if zz < 2:
                self.across(zz + 2).wait_send()
            self.out[zz % 2] = value
            self.across(zz).start()

    def place(self, zz):
        return jnp.where(self.half == 0, zz, 3 - zz)

    def part(self, side):
        rows = self.fin.shape[0] // 2
        return pl.ds(side * rows, rows)

    def to_partner(self, zz, side):
        rows = self.part(side)
        return remote(
            self.mine.at[zz, rows], self.got.at[zz, rows], self.send.at[zz, side], self.recv.at[zz, side], self.partner
        )

    def to_owner(self, zz, side):
        rows = self.part(side)
        return remote(
            self.mine.at[zz, rows], self.fin.at[rows], self.on_send.at[zz, side], self.fin_recv.at[side],
            at(zz, self.core, self.y, self.x),
        )

    def sends_to_partner(self, zz):
        place = self.place(zz)
        return jnp.where(self.near == 0, place != 0, place == 0)

    def add_cores(self, zz):
        self.across(zz).wait_recv()
        for side in range(2):
            rows = self.part(side)
            add_into(self.mine.at[zz, rows], self.sib.at[zz, rows])
            pl.when(self.sends_to_partner(zz))(self.to_partner(zz, side).start)

    def sends_on(self, zz):
        return jnp.logical_and(self.near == 1, self.place(zz) >= 2)

    def add_chips(self, zz):
        @pl.when(self.sends_on(zz))
        def _():
            for side in range(2):
                rows = self.part(side)
                self.to_partner(zz, side).wait_recv()
                add_into(self.mine.at[zz, rows], self.got.at[zz, rows])
                self.to_owner(zz, side).start()

    def across_s(self, zz):
        return remote(
            self.out_s.at[zz], self.sib_s.at[zz], self.sib_send_s.at[zz], self.sib_recv_s.at[zz], self.sibling
        )

    def put_short(self, zz, value):
        rows = value.shape[0] // 2
        first, second = value[:rows], value[rows:]

        @pl.when(self.core == 0)
        def _():
            self.mine_s[zz] = first
            self.out_s[zz] = second

        @pl.when(self.core == 1)
        def _():
            self.mine_s[zz] = second
            self.out_s[zz] = first

        self.across_s(zz).start()

    def to_owner_s(self, zz):
        return remote(
            self.mine_s.at[zz], self.fin_s.at[self.half], self.send_s.at[zz], self.fin_recv_s.at[self.half],
            at(zz, self.core, self.y, self.x),
        )

    def add_short(self, zz):
        @pl.when(self.near == 1)
        def _():
            self.across_s(zz).wait_recv()
            add_into(self.mine_s.at[zz], self.sib_s.at[zz])
            pl.when(self.z != zz)(self.to_owner_s(zz).start)

    def own_long(self):
        for side in range(2):
            self.to_partner(self.z, side).wait_recv()
        return self.mine[self.z].astype(F32) + self.got[self.z].astype(F32)

    def other_long(self):
        for side in range(2):
            block = self.fin.at[self.part(side)]
            remote(block, block, self.on_send.at[0, 0], self.fin_recv.at[side], self.far).wait_recv()
        return self.fin[...].astype(F32)

    def shorts(self):
        def arrival(seq):
            block = self.fin_s.at[seq]
            remote(block, block, self.send_s.at[0], self.fin_recv_s.at[seq], self.far).wait_recv()

        arrival(1 - self.half)
        pl.when(self.near == 0)(lambda: arrival(self.half))

        @pl.when(self.near == 1)
        def _():
            self.fin_s[self.half] = self.mine_s[self.z]

    def sends_done(self):
        for zz in range(4):
            if zz < 2:
                self.across(zz).wait_send()
            for side in range(2):
                pl.when(self.sends_to_partner(zz))(self.to_partner(zz, side).wait_send)
                pl.when(self.sends_on(zz))(self.to_owner(zz, side).wait_send)

        @pl.when(self.near == 1)
        def _():
            for zz in range(4):
                self.across_s(zz).wait_send()
                pl.when(self.z != zz)(self.to_owner_s(zz).wait_send)


def third_kernel(
    xs_own, xl_own, gnorm, wq, taps, norms, gmid,
    xs_h, xl_h, ql_h, kl_h, vl_h, ktl_h, lsel_h, pl_h, ol_h, qs_h, ks_h, vs_h, kts_h, lses_h, ps_h, os_h,
    gl_h, gs_h, gwo_h, gwu_h, gwd_h,
    dxs_ref, dxl_ref, gwq_ref, gwo_ref, gwu_ref, gwd_ref, small_ref,
    ql, kl, vl, ktl, lsel, ol, gl, qs, ks, vs, kts, lses, os, gs,
    gm, dqt, delta, gp, early_gn, dwq, dtaps, dnorms, x_tile, p_tile,
    mine, out, sib, got, fin, mine_s, out_s, sib_s, fin_s,
    load_sem, tile_sem,
    r0, r1, r2, r3, r4, r5, r6, r7, r8, r9,
    shard_own, shard_send, shard_recv, group_send, group_recv, small_send, small_recv,
    *bufs,
):
    z, core, y, x = position()
    half, near, _, _ = roles()
    long_moves = (
        (ql_h, ql), (kl_h, kl), (vl_h, vl), (ktl_h, ktl), (lsel_h, lsel), (ol_h, ol), (gl_h, gl),
    )
    short_moves = (
        (qs_h, qs), (ks_h, ks), (vs_h, vs), (kts_h, kts), (lses_h, lses), (os_h, os), (gs_h, gs),
    )
    loads = [
        pltpu.make_async_copy(source, target, load_sem.at[i])
        for i, (source, target) in enumerate(long_moves + short_moves)
    ]
    long_loads, short_loads = loads[:7], loads[7:]

    @pl.when(near == 1)
    def _():
        for copy in short_loads:
            copy.start()

    for copy in long_loads:
        copy.start()
    greet_all()
    bufs = list(bufs)
    sums = []
    for i, (grad, total, begun) in enumerate(
        ((gwo_h, gwo_ref, False), (gwu_h, gwu_ref, False), (gwd_h, gwd_ref, False))
    ):
        size = 4 if begun else 5
        mine_bufs, bufs = bufs[:size], bufs[size:]
        sums.append(ShardSum(grad, total, mine_bufs, shard_own.at[i], shard_send.at[i], shard_recv.at[i], begun))
    group_early = GroupSum(bufs[0:4], group_send.at[0], group_recv.at[0])
    group_late = GroupSum(bufs[4:8], group_send.at[1], group_recv.at[1])
    small = SmallSum(bufs[8:13], small_ref, small_send, small_recv)
    rows_sum = RowSum((mine, out, sib, got, fin), (mine_s, out_s, sib_s, fin_s), (r0, r1, r2, r3, r4, r5, r6, r7, r8, r9))
    sum_out, sum_up, sum_down = sums
    sum_up.start()
    short, long = xs_own.shape[1], xl_own.shape[1]
    middles = [
        pltpu.make_async_copy(gmid.at[pl.ds(first + seq * size, size)], dx.at[seq], load_sem.at[14 + 2 * seq + i])
        for seq in range(2)
        for i, (dx, first, size) in enumerate(((dxs_ref, 2 * long, short), (dxl_ref, 0, long)))
    ]
    for copy in middles:
        copy.start()
    gm[...] = jnp.zeros_like(gm)
    dwq[...] = jnp.zeros_like(dwq)
    dtaps[...] = jnp.zeros_like(dtaps)
    dnorms[...] = gnorm[...]
    gain, offset = norms[0:1], norms[1:2]
    causal = causal_mask()
    first_lanes = iota((TILE, LANES), 1) < HEAD_DIM

    def back_head(refs, grad_ref, slot, side, local, block):
        q_ref, k_ref, v_ref, kt_ref, lse, _, g_ref = refs
        head = 2 * slot + side
        own_lanes = first_lanes == (side == 0)
        rows = slice(block * TILE, (block + 1) * TILE)
        query = q_ref[head, rows]
        bare = jnp.where(own_lanes, query.astype(F32), 0.0).astype(BF16)
        grad_out = jnp.where(own_lanes, g_ref[slot, rows].astype(F32), 0.0).astype(BF16)
        stat, less = lse[head, :, rows], delta[local]
        spans = [(block * TILE, TILE, True)]
        if block:
            spans.append((0, block * TILE, False))
        grad_q = None
        for start, size, masked in spans:
            keys = slice(start, start + size)
            scores = dot_nt(k_ref[head, keys], query)
            if masked:
                scores = jnp.where(causal, scores, NEG_FILL)
            probs = jnp.exp(scores - stat)
            grad_probs = dot_nt(v_ref[slot, keys], grad_out)
            grad_ref[keys, 2 * LANES :] += dot_nn(probs.astype(BF16), grad_out)
            grad_scores = (probs * (grad_probs - less)).astype(BF16)
            grad_ref[keys, LANES : 2 * LANES] += dot_nn(grad_scores, bare)
            term = dot_nn(kt_ref[head, :, keys], grad_scores)
            grad_q = term if grad_q is None else grad_q + term
        dqt[local] = (HEAD_DIM**-0.5) * grad_q

    def back_block(refs, x_h, p_h, count, first_slot, first_pair, block):
        o_ref, g_ref = refs[5], refs[6]
        rows = slice(block * TILE, (block + 1) * TILE)
        span = x_h.shape[0] + PAD
        got_x = pltpu.make_async_copy(x_h.at[pl.ds(block * TILE, TILE)], x_tile, tile_sem.at[0])
        got_p = pltpu.make_async_copy(
            p_h.at[pl.ds(first_slot, count), pl.ds(block * TILE, TILE + PAD)], p_tile.at[pl.ds(0, count)], tile_sem.at[1]
        )
        got_x.start()
        got_p.start()
        for local in range(count):
            product = g_ref[first_slot + local, rows].astype(F32) * o_ref[first_slot + local, rows].astype(F32)
            turned = product.T
            delta[2 * local] = jnp.sum(turned[:HEAD_DIM], axis=0, keepdims=True)
            delta[2 * local + 1] = jnp.sum(turned[HEAD_DIM:], axis=0, keepdims=True)

        @pl.loop(0, 2 * count)
        def _(local):
            slot = local // 2
            grad_ref = gm.at[pl.ds(pl.multiple_of(slot * span, PAD), span)]
            back_head(refs, grad_ref, first_slot + slot, local % 2, local, block)

        got_x.wait()
        got_p.wait()
        normal, _ = normalise(x_tile[...].astype(F32))
        low = (normal * gain + offset).astype(BF16)
        for local in range(count):
            grad_ref = gm.at[pl.ds(local * span, span)]
            grad_ref[rows, 0:LANES] = jnp.concatenate([dqt[2 * local], dqt[2 * local + 1]], axis=0).T
            window = grad_ref[pl.ds(block * TILE, TILE + PAD)]
            grad = window[:TILE]
            columns = pl.ds(pl.multiple_of((first_pair + local) * TRIPLE, TRIPLE), TRIPLE)
            kernel = taps[:, columns]
            grad_projected = (
                kernel[0:1] * grad + kernel[1:2] * shifted(window, -1)[:TILE] + kernel[2:3] * shifted(window, -2)[:TILE]
            ).astype(BF16)
            past = p_tile[local].astype(F32)
            dtaps[0:1, columns] += jnp.sum(grad * past[PAD:], axis=0, keepdims=True)
            dtaps[1:2, columns] += jnp.sum(grad * shifted(past, 1)[PAD:], axis=0, keepdims=True)
            dtaps[2:3, columns] += jnp.sum(grad * shifted(past, 2)[PAD:], axis=0, keepdims=True)
            gp[:, local * TRIPLE : (local + 1) * TRIPLE] = grad_projected
        grads = gp[:, : count * TRIPLE]
        columns = pl.ds(pl.multiple_of(first_pair * TRIPLE, TRIPLE), count * TRIPLE)
        grad_normed = dot_nt(grads, wq[:, columns])
        dwq[:, columns] += dot_tn(low, grads)
        dnorms[0:1] += jnp.sum(grad_normed * normal, axis=0, keepdims=True)
        dnorms[1:2] += jnp.sum(grad_normed, axis=0, keepdims=True)
        return grad_normed

    def hook_one():
        sum_up.turn()
        sum_down.start()
        sum_out.start()

    def hook_two():
        sum_up.last()

    def hook_three():
        sum_down.turn()
        sum_out.turn()

    def hook_four():
        sum_down.last()
        sum_out.last()

    def finish_rows(seq, grad, x_ref, dx_ref):
        normal, inverse = normalise(x_ref[seq].astype(F32))
        dx_ref[seq] += norm_back(grad, normal, inverse, gain)

    long_refs = (ql, kl, vl, ktl, lsel, ol, gl)
    short_refs = (qs, ks, vs, kts, lses, os, gs)
    last_long = xl_h.shape[0] // TILE - 1
    last_short = xs_h.shape[0] // TILE - 1

    @pl.when(near == 0)
    def _():
        for copy in long_loads:
            copy.wait()
        for block in range(last_long, -1, -1):
            value = back_block(long_refs, xl_h, pl_h, 1, 0, 0, block)
            early_gn[block * TILE : (block + 1) * TILE] = value.astype(BF16)
            if block == 6:
                hook_one()
            if block == 3:
                hook_two()

    @pl.when(near == 1)
    def _():
        for copy in short_loads:
            copy.wait()
        for block in range(last_short, -1, -1):
            value = back_block(short_refs, xs_h, ps_h, 3, 0, 0, block)
            rows_sum.put_short(block, value.astype(BF16))
            if block == 3:
                hook_one()
            if block == 1:
                hook_two()
        for copy in long_loads:
            copy.wait()

    hook_three()
    group_early.start(dwq, pl.ds(0, 2 * TRIPLE))
    gm[...] = jnp.zeros_like(gm)

    for block in range(last_long, -1, -1):
        value = back_block(long_refs, xl_h, pl_h, 1, 1 - near, 1 + near, block)
        early = early_gn[block * TILE : (block + 1) * TILE].astype(F32)
        rows_sum.put(block, (value + jnp.where(near == 0, early, 0.0)).astype(BF16))
        if block % 2 == 1 and block != last_long:
            rows_sum.add_cores(block // 2 + 1)
        if block > 3:
            rows_sum.add_short(block - 4)
        if block == 7:
            hook_four()
        if block == 6:
            group_early.turn()
        if block == 5:
            group_early.last()
        if block == 2:
            rows_sum.add_chips(3)
    group_late.start(dwq, pl.ds(pl.multiple_of((1 + near) * TRIPLE, TRIPLE), TRIPLE))
    small.start(dtaps[...], dnorms[...])
    rows_sum.add_cores(0)
    rows_sum.add_chips(2)
    small.over()
    group_late.turn()
    rows_sum.add_chips(1)
    small.turn()
    for copy in middles:
        copy.wait()
    rows_sum.shorts()
    finish_rows(half, rows_sum.fin_s[half].astype(F32), xs_own, dxs_ref)
    group_late.last()
    small.last()
    rows_sum.add_chips(0)
    finish_rows(1 - half, rows_sum.fin_s[1 - half].astype(F32), xs_own, dxs_ref)
    finish_rows(half, rows_sum.own_long(), xl_own, dxl_ref)
    for one in sums:
        one.finish()
    group_early.finish()
    small.swap_back()
    group_late.finish()
    join_groups(group_early, group_late, gwq_ref)
    finish_rows(1 - half, rows_sum.other_long(), xl_own, dxl_ref)
    small.finish()
    rows_sum.sends_done()


def third_part(x_short, x_long, gmid, gnorm, wq, taps, norms, kept, grads_in, weight_grads):
    width = x_short.shape[2]
    wide = wq.shape[1]
    count = 8
    short, long = count * x_short.shape[1], count * x_long.shape[1]
    own_short = x_short.shape[1]
    rows = weight_grads[0].shape[3]
    out = jax.ShapeDtypeStruct
    small_wide = wide + width // 2

    def saved(pairs, total):
        return [
            ((2 * pairs, total, LANES), BF16),
            ((2 * pairs, total, LANES), BF16),
            ((pairs, total, LANES), BF16),
            ((2 * pairs, HEAD_DIM, total), BF16),
            ((2 * pairs, 1, total), F32),
            ((pairs, total, LANES), BF16),
            ((pairs, total, LANES), BF16),
        ]

    scratch = (
        saved(2, long)
        + saved(3, short)
        + [
            ((max(long + PAD, 3 * (short + PAD)), TRIPLE), F32),
            ((6, HEAD_DIM, TILE), F32),
            ((6, 1, TILE), F32),
            ((TILE, wide), BF16),
            ((long, width), BF16),
            ((width, wide), F32),
            ((8, wide), F32),
            ((8, width), F32),
            ((TILE, width), BF16),
            ((3, TILE + PAD, TRIPLE), BF16),
        ]
        + [((4, TILE, width), BF16), ((2, TILE, width), BF16)]
        + [((4, TILE, width), BF16)] * 2
        + [((TILE, width), BF16)]
        + [((4, own_short, width), BF16)] * 3
        + [((2, own_short, width), BF16)]
    )
    buffers = []
    for i, g in enumerate(weight_grads):
        buffers += ShardSum.buffers(g)
    buffers += GroupSum.buffers(rows, 2 * TRIPLE) + GroupSum.buffers(rows, TRIPLE) + SmallSum.buffers(wide, width // 2)
    return pl.pallas_call(
        third_kernel,
        out_shape=(
            out(x_short.shape, F32),
            out(x_long.shape, F32),
            out((rows, 2 * wide), F32),
            *[out(g.shape[3:], F32) for g in weight_grads],
            out((2, 8, small_wide), F32),
        ),
        in_specs=[vmem()] * 6 + [hbm()] * (1 + len(kept) + len(grads_in) + len(weight_grads)),
        out_specs=tuple([vmem()] * 7),
        scratch_shapes=[pltpu.VMEM(*one) for one in scratch]
        + [DMA((18,)), DMA((2,))]
        + [DMA((4,))] * 2 + [DMA((4, 2))] * 3 + [DMA((2,))] + [DMA((4,))] * 3 + [DMA((2,))]
        + [DMA((3, 2)), DMA((3, 9)), DMA((3, 9)), DMA((2, 11)), DMA((2, 11)), DMA((7,)), DMA((7,))]
        + buffers,
        compiler_params=params_of(63, collective_id=2, has_side_effects=True),
    )(x_short, x_long, gnorm, wq, taps, norms, gmid, *kept, *grads_in, *weight_grads)


def last_kernel(*refs):
    *arrays, smalls = refs[:9]
    outs, kernel_out, norm_out = refs[9:17], refs[17], refs[18]
    held, sems = refs[19:27], refs[27]
    loads = [pltpu.make_async_copy(a, h, sems.at[0, i]) for i, (a, h) in enumerate(zip(arrays, held))]
    copies = [pltpu.make_async_copy(h, o, sems.at[1, i]) for i, (h, o) in enumerate(zip(held, outs))]
    for copy in loads:
        copy.start()
    number = lax.axis_index("seq") * lax.axis_size("batch") + lax.axis_index("batch")
    (taps, part), (norms, cut) = kernel_out.shape, norm_out.shape
    norm_columns = norm_out.shape[1] * 32 // 2
    wide = smalls.shape[2] - norm_columns
    width = 2 * wide // 3

    def pick(values, source, first):
        chosen = jnp.where(source == first + iota(source.shape, 1), 1.0, 0.0)
        return lax.dot_general(
            values, chosen, (((1,), (0,)), ((), ())), preferred_element_type=F32, precision=lax.Precision.HIGHEST
        )

    row = iota((wide, LANES), 0)
    block = row // LANES
    norm_row = iota((norm_columns, LANES), 0)
    kernel_sum, norm_sum = None, None
    for load, copy in zip(loads, copies):
        load.wait()
        copy.start()
    for side in range(2):
        source = (block % 3) * width + (3 * side + block // 3) * LANES + row % LANES
        term = pick(smalls[side, :, :wide], source, number * part)
        norm_term = pick(smalls[side, :, wide:], norm_row + side * norm_columns, number * cut)
        kernel_sum = term if side == 0 else kernel_sum + term
        norm_sum = norm_term if side == 0 else norm_sum + norm_term
    kernel_out[...] = kernel_sum[:taps, :part]
    norm_out[...] = norm_sum[:norms, :cut]
    for copy in copies:
        copy.wait()


def last_part(arrays, smalls, taps, part, cut):
    out = jax.ShapeDtypeStruct
    return pl.pallas_call(
        last_kernel,
        out_shape=(*[out(a.shape, a.dtype) for a in arrays], out((taps, part), F32), out((4, cut), F32)),
        in_specs=[hbm()] * 8 + [vmem()],
        out_specs=tuple([hbm()] * 8 + [vmem()] * 2),
        scratch_shapes=[pltpu.VMEM(a.shape, a.dtype) for a in arrays] + [DMA((2, 8))],
        compiler_params=params_of(),
    )(*arrays, smalls)


def split_body(
    x_short, x_long, lengths, cot_short, cot_long, w_qkv, w_out, w_up, w_down, conv_kernel, norm_params
):
    count = lax.axis_size("seq")
    width = x_short.shape[2]
    att, full_out, full_up, full_down, xs, xl, wq, taps, norms, *kept = first_part(
        lengths, x_short, x_long, w_qkv, conv_kernel, norm_params, w_out, w_up, w_down, count
    )
    y_short, y_long, gmid, gnorm, gwo, gwu, gwd, gl, gs = second_part(
        x_short, x_long, att, cot_short, cot_long, norms,
        full_out.reshape(width, -1), full_up.reshape(width, -1), full_down.reshape(-1, width), count,
    )
    dx_short, dx_long, sum_qkv, sum_out, sum_up, sum_down, smalls = third_part(
        x_short, x_long, gmid, gnorm, wq, taps, norms, [xs, xl] + kept, [gl, gs], [gwo, gwu, gwd]
    )
    return last_part(
        (y_short, y_long, dx_short, dx_long, sum_qkv, sum_out, sum_up, sum_down), smalls,
        conv_kernel.shape[0], conv_kernel.shape[1], norm_params.shape[1],
    )


GROUP_HEADS = 2


def from_behind(value, axis, by):
    count = lax.axis_size(axis)
    pairs = [(i, i + by) for i in range(count) if 0 <= i + by < count]
    return lax.ppermute(value, axis, pairs)


def layer_norm(values, gain, offset_term):
    average = jnp.mean(values, axis=-1, keepdims=True)
    centred = values - average
    inverse = lax.rsqrt(jnp.mean(centred * centred, axis=-1, keepdims=True) + EPS)
    normal = centred * inverse
    return (normal * gain + offset_term, normal, inverse)


def norm_back_flat(grad, normal, inverse, gain):
    scaled_grad = grad * gain
    first_mean = jnp.mean(scaled_grad, axis=-1, keepdims=True)
    second_mean = jnp.mean(scaled_grad * normal, axis=-1, keepdims=True)
    return inverse * (scaled_grad - first_mean - normal * second_mean)


def front_part(inputs, full_weights):
    w_qkv = full_weights[0]
    kernel = full_weights[4].astype(jnp.float32)
    params = full_weights[5].astype(jnp.float32)
    saved = []
    tails = []
    for part_in in inputs:
        seq_count, block_rows, model_width = part_in.shape
        flat = part_in.reshape(seq_count * block_rows, model_width).astype(jnp.float32)
        normed, normal, inverse = layer_norm(flat, params[0], params[1])
        normed_low = normed.astype(jnp.bfloat16)
        projected = jnp.dot(normed_low, w_qkv, preferred_element_type=jnp.float32).astype(
            jnp.bfloat16
        )
        projected = projected.reshape(seq_count, block_rows, 3 * model_width)
        saved.append((flat, normal, inverse, normed_low, projected))
        tails.append(projected[:, block_rows - 2 :])
    received = from_behind((tails[0], tails[1]), "seq", 1)
    fronts = []
    for index_part in range(2):
        flat, normal, inverse, normed_low, projected = saved[index_part]
        block_rows = projected.shape[1]
        padded = jnp.concatenate([received[index_part], projected], axis=1).astype(jnp.float32)
        mixed = (
            kernel[0] * padded[:, 2:]
            + kernel[1] * padded[:, 1 : block_rows + 1]
            + kernel[2] * padded[:, :block_rows]
        )
        fronts.append((flat, normal, inverse, normed_low, padded, mixed.astype(jnp.bfloat16)))
    return fronts


def attend_block(queries, key_rows, value_rows, usable, grad_heads):
    scaling = queries.shape[-1] ** (-0.5)
    scores = jnp.einsum("sqhd,skhd->shqk", queries, key_rows, preferred_element_type=jnp.float32)
    masked = jnp.where(usable, scaling * scores, NEG_FILL)
    exp_terms = jnp.exp(masked - jnp.max(masked, axis=-1, keepdims=True))
    attn_probs = exp_terms / jnp.sum(exp_terms, axis=-1, keepdims=True)
    probs_low = attn_probs.astype(jnp.bfloat16)
    if grad_heads is None:
        attended = jnp.einsum(
            "shqk,skhd->sqhd", probs_low, value_rows, preferred_element_type=jnp.float32
        )
        return attended.astype(jnp.bfloat16)
    grad_probs = jnp.einsum(
        "sqhd,skhd->shqk", grad_heads, value_rows, preferred_element_type=jnp.float32
    )
    grad_values = jnp.einsum(
        "shqk,sqhd->skhd", probs_low, grad_heads, preferred_element_type=jnp.float32
    )
    row_delta = jnp.sum(attn_probs * grad_probs, axis=-1, keepdims=True)
    grad_scores = (scaling * attn_probs * (grad_probs - row_delta)).astype(jnp.bfloat16)
    grad_queries = jnp.einsum(
        "shqk,skhd->sqhd", grad_scores, key_rows, preferred_element_type=jnp.float32
    )
    grad_keys = jnp.einsum(
        "shqk,sqhd->skhd", grad_scores, queries, preferred_element_type=jnp.float32
    )
    return (grad_queries, grad_keys, grad_values)


def make_usable(query_pos, key_pos, seq_lengths):
    usable = (key_pos[None, None, :] <= query_pos[None, :, None]) & (
        key_pos[None, None, :] < seq_lengths[:, None, None]
    )
    return usable[:, None]


def attention(mixed, kv_full, seq_lengths, offset, grad_attended):
    seq_count, block_rows, three_width = mixed.shape
    model_width = three_width // 3
    full_len = kv_full.shape[1]
    queries = mixed[:, :, :model_width].reshape(seq_count, block_rows, -1, HEAD_DIM)
    key_rows = kv_full[:, :, :model_width].reshape(seq_count, full_len, -1, HEAD_DIM)
    value_rows = kv_full[:, :, model_width:].reshape(seq_count, full_len, -1, HEAD_DIM)
    positions = offset + jnp.arange(block_rows, dtype=jnp.int32)
    key_pos = jnp.arange(full_len, dtype=jnp.int32)
    usable = make_usable(positions, key_pos, seq_lengths)
    heads_total = queries.shape[2]
    grad_heads = None
    if grad_attended is not None:
        grad_heads = grad_attended.reshape(seq_count, block_rows, -1, HEAD_DIM)
    results = []
    for first_head in range(0, heads_total, GROUP_HEADS):
        last_head = first_head + GROUP_HEADS
        grad_part = None if grad_heads is None else grad_heads[:, :, first_head:last_head]
        results.append(
            attend_block(
                queries[:, :, first_head:last_head],
                key_rows[:, :, first_head:last_head],
                value_rows[:, :, first_head:last_head],
                usable,
                grad_part,
            )
        )
    if grad_heads is None:
        return jnp.concatenate(results, axis=2).reshape(seq_count, block_rows, model_width)
    grad_queries = jnp.concatenate([entry_set[0] for entry_set in results], axis=2).reshape(
        seq_count, block_rows, model_width
    )
    grad_keys = jnp.concatenate([entry_set[1] for entry_set in results], axis=2).reshape(
        seq_count, full_len, model_width
    )
    grad_values = jnp.concatenate([entry_set[2] for entry_set in results], axis=2).reshape(
        seq_count, full_len, model_width
    )
    return (grad_queries, grad_keys, grad_values)


def rest_part(front, kv_full, seq_lengths, offset, full_weights, cotangent_in):
    w_out, w_up, w_down = (full_weights[1], full_weights[2], full_weights[3])
    params = full_weights[5].astype(jnp.float32)
    flat, normal_one, inverse_one, normed_low, padded, mixed = front
    seq_count, block_rows, three_width = mixed.shape
    model_width = three_width // 3
    attended = attention(mixed, kv_full, seq_lengths, offset, None).reshape(
        seq_count * block_rows, model_width
    )
    middle = flat + jnp.dot(attended, w_out, preferred_element_type=jnp.float32)
    second, normal_two, inverse_two = layer_norm(middle, params[2], params[3])
    second_low = second.astype(jnp.bfloat16)
    upper = jnp.dot(second_low, w_up, preferred_element_type=jnp.float32)
    hidden = jnp.square(jnp.maximum(upper, 0.0)).astype(jnp.bfloat16)
    if cotangent_in is None:
        result_rows = middle + jnp.dot(hidden, w_down, preferred_element_type=jnp.float32)
        return result_rows.astype(jnp.bfloat16).reshape(seq_count, block_rows, model_width)
    cotangent = cotangent_in.reshape(seq_count * block_rows, model_width)
    grad_down = jnp.dot(hidden.T, cotangent, preferred_element_type=jnp.float32)
    grad_hidden = jnp.dot(cotangent, w_down.T, preferred_element_type=jnp.float32)
    grad_upper = (2.0 * jnp.maximum(upper, 0.0) * grad_hidden).astype(jnp.bfloat16)
    grad_up = jnp.dot(second_low.T, grad_upper, preferred_element_type=jnp.float32)
    grad_second = jnp.dot(grad_upper, w_up.T, preferred_element_type=jnp.float32)
    grad_middle = cotangent.astype(jnp.float32) + norm_back_flat(
        grad_second, normal_two, inverse_two, params[2]
    )
    grad_middle_low = grad_middle.astype(jnp.bfloat16)
    grad_out = jnp.dot(attended.T, grad_middle_low, preferred_element_type=jnp.float32)
    grad_attended = jnp.dot(grad_middle_low, w_out.T, preferred_element_type=jnp.float32).astype(
        jnp.bfloat16
    )
    grad_attended = grad_attended.reshape(seq_count, block_rows, model_width)
    grad_queries, grad_keys, grad_values = attention(
        mixed, kv_full, seq_lengths, offset, grad_attended
    )
    key_term = jnp.concatenate([grad_keys, grad_values], axis=-1)
    norm_two = (jnp.sum(grad_second * normal_two, axis=0), jnp.sum(grad_second, axis=0))
    return (grad_queries, key_term, grad_middle, grad_out, grad_up, grad_down, norm_two)


def general_body(
    x_short,
    x_long,
    lengths,
    cot_short,
    cot_long,
    w_qkv,
    w_out,
    w_up,
    w_down,
    conv_kernel,
    norm_params,
):
    full_weights = (
        lax.all_gather(w_qkv, ("seq", "batch"), axis=0, tiled=True),
        lax.all_gather(w_out, ("seq", "batch"), axis=0, tiled=True),
        lax.all_gather(w_up, ("seq", "batch"), axis=0, tiled=True),
        lax.all_gather(w_down, ("seq", "batch"), axis=0, tiled=True),
        lax.all_gather(conv_kernel, ("seq", "batch"), axis=1, tiled=True),
        lax.all_gather(norm_params, ("seq", "batch"), axis=1, tiled=True),
    )
    inputs = (x_short, x_long)
    cotangents = (cot_short, cot_long)
    model_width = x_short.shape[2]
    offsets = (lax.axis_index("seq") * x_short.shape[1], lax.axis_index("seq") * x_long.shape[1])
    fronts = front_part(inputs, full_weights)
    kv_fwd = (
        lax.all_gather(fronts[0][5][:, :, model_width:], "seq", axis=1, tiled=True),
        lax.all_gather(fronts[1][5][:, :, model_width:], "seq", axis=1, tiled=True),
    )
    outputs = [
        rest_part(
            fronts[index_part],
            kv_fwd[index_part],
            lengths[index_part],
            offsets[index_part],
            full_weights,
            None,
        )
        for index_part in range(2)
    ]
    back_weights = (
        lax.all_gather(w_qkv, ("seq", "batch"), axis=0, tiled=True),
        lax.all_gather(w_out, ("seq", "batch"), axis=0, tiled=True),
        lax.all_gather(w_up, ("seq", "batch"), axis=0, tiled=True),
        lax.all_gather(w_down, ("seq", "batch"), axis=0, tiled=True),
        lax.all_gather(conv_kernel, ("seq", "batch"), axis=1, tiled=True),
        lax.all_gather(norm_params, ("seq", "batch"), axis=1, tiled=True),
    )
    fronts_back = front_part(inputs, back_weights)
    kv_back = (
        lax.all_gather(fronts_back[0][5][:, :, model_width:], "seq", axis=1, tiled=True),
        lax.all_gather(fronts_back[1][5][:, :, model_width:], "seq", axis=1, tiled=True),
    )
    partials = [
        rest_part(
            fronts_back[index_part],
            kv_back[index_part],
            lengths[index_part],
            offsets[index_part],
            back_weights,
            cotangents[index_part],
        )
        for index_part in range(2)
    ]
    kv_grads = (
        lax.psum_scatter(
            partials[0][1].astype(jnp.bfloat16), "seq", scatter_dimension=1, tiled=True
        ).astype(jnp.float32),
        lax.psum_scatter(
            partials[1][1].astype(jnp.bfloat16), "seq", scatter_dimension=1, tiled=True
        ).astype(jnp.float32),
    )
    grad_mixed = [
        jnp.concatenate([partials[index_part][0], kv_grads[index_part]], axis=-1)
        for index_part in range(2)
    ]
    received = (
        from_behind(grad_mixed[0][:, :2].astype(jnp.bfloat16), "seq", -1).astype(jnp.float32),
        from_behind(grad_mixed[1][:, :2].astype(jnp.bfloat16), "seq", -1).astype(jnp.float32),
    )
    kernel = back_weights[4].astype(jnp.float32)
    params = back_weights[5].astype(jnp.float32)
    w_qkv_full = back_weights[0]
    grad_qkv = jnp.zeros(w_qkv_full.shape, jnp.float32)
    grad_kernel = jnp.zeros(kernel.shape, jnp.float32)
    grad_norm = jnp.zeros((4, model_width), jnp.float32)
    grad_out = partials[0][3] + partials[1][3]
    grad_up = partials[0][4] + partials[1][4]
    grad_down = partials[0][5] + partials[1][5]
    input_grads = []
    for index_part in range(2):
        flat, normal_one, inverse_one, normed_low, padded, mixed = fronts_back[index_part]
        seq_count, block_rows, three_width = mixed.shape
        mixed_grad = grad_mixed[index_part]
        extended = jnp.concatenate([mixed_grad, received[index_part]], axis=1)
        grad_projected = (
            kernel[0] * extended[:, :block_rows]
            + kernel[1] * extended[:, 1 : block_rows + 1]
            + kernel[2] * extended[:, 2:]
        ).astype(jnp.bfloat16)
        grad_kernel = grad_kernel + jnp.stack(
            [
                jnp.sum(mixed_grad * padded[:, 2:], axis=(0, 1)),
                jnp.sum(mixed_grad * padded[:, 1 : block_rows + 1], axis=(0, 1)),
                jnp.sum(mixed_grad * padded[:, :block_rows], axis=(0, 1)),
            ]
        )
        grad_flat = grad_projected.reshape(seq_count * block_rows, three_width)
        grad_qkv = grad_qkv + jnp.dot(normed_low.T, grad_flat, preferred_element_type=jnp.float32)
        grad_normed = jnp.dot(grad_flat, w_qkv_full.T, preferred_element_type=jnp.float32)
        grad_input = partials[index_part][2] + norm_back_flat(
            grad_normed, normal_one, inverse_one, params[0]
        )
        input_grads.append(grad_input.reshape(seq_count, block_rows, model_width))
        norm_two = partials[index_part][6]
        grad_norm = grad_norm + jnp.stack(
            [
                jnp.sum(grad_normed * normal_one, axis=0),
                jnp.sum(grad_normed, axis=0),
                norm_two[0],
                norm_two[1],
            ]
        )
    summed = (
        lax.psum_scatter(grad_qkv, ("seq", "batch"), scatter_dimension=0, tiled=True),
        lax.psum_scatter(grad_out, ("seq", "batch"), scatter_dimension=0, tiled=True),
        lax.psum_scatter(grad_up, ("seq", "batch"), scatter_dimension=0, tiled=True),
        lax.psum_scatter(grad_down, ("seq", "batch"), scatter_dimension=0, tiled=True),
        lax.psum_scatter(grad_kernel, ("seq", "batch"), scatter_dimension=1, tiled=True),
        lax.psum_scatter(grad_norm, ("seq", "batch"), scatter_dimension=1, tiled=True),
    )
    return (
        outputs[0],
        outputs[1],
        input_grads[0],
        input_grads[1],
        summed[0],
        summed[1],
        summed[2],
        summed[3],
        summed[4],
        summed[5],
    )


def solution(mesh):
    split = mesh.shape["seq"] == 8
    return jax.shard_map(
        split_body if split else general_body,
        mesh=mesh,
        in_specs=(
            P("batch", "seq", None),
            P("batch", "seq", None),
            P(None, "batch"),
            P("batch", "seq", None),
            P("batch", "seq", None),
            P(("seq", "batch"), None),
            P(("seq", "batch"), None),
            P(("seq", "batch"), None),
            P(("seq", "batch"), None),
            P(None, ("seq", "batch")),
            P(None, ("seq", "batch")),
        ),
        out_specs=(
            P("batch", "seq", None),
            P("batch", "seq", None),
            P("batch", "seq", None),
            P("batch", "seq", None),
            P(("seq", "batch"), None),
            P(("seq", "batch"), None),
            P(("seq", "batch"), None),
            P(("seq", "batch"), None),
            P(None, ("seq", "batch")),
            P(None, ("seq", "batch")),
        ),
        check_vma=False,
    )
```

profile of v0, /device:TPU:0, one launch (start us, length us, event | category | flops | bytes accessed | tf_op | source)
XLA Modules:
  0.0 303.6 jit_solution(13087421592235800767)
XLA Ops:
  0.6 129.2 %shard_map.186 = (bf16[768,768]{1,0:T(8,128)(2,1)}, bf16[4,2,2,2,24,768]{5,4,3,2,1,0:T(8,128)(2,1)}, bf16[4,2,2,2,24,3072]{5,4,3,2,1,0:T(8,128)(2,1)}, bf16[4,2,...) custom-call(s32[2,2]{1,0:T(2,128)} %lens.1, ...), custom_call_target="tpu_custom_call" | custom-call | tf_op jit(solution)/shard_map/pallas_call | solution.py:1052
  129.9 45.3 %shard_map.187 = (bf16[2,128,768]{2,1,0:T(8,128)(2,1)}, bf16[2,256,768]{2,1,0:T(8,128)(2,1)}, f32[768,768]{1,0:T(8,128)}, f32[8,768]{1,0:T(8,128)}, bf16[4,2,2,2...) custom-call(bf16[2,128,768]{2,1,0:T(8,128)(2,1)} %xs_own.1, ...), custom_call_target="tpu_custom_call" | custom-call | tf_op jit(solution)/shard_map/pallas_call | solution.py:1238
  175.2 122.4 %shard_map.188 = (f32[2,128,768]{2,1,0:T(8,128)}, f32[2,256,768]{2,1,0:T(8,128)}, f32[24,2304]{1,0:T(8,128)}, f32[24,768]{1,0:T(8,128)}, f32[24,3072]{1,0:T(8,12...) custom-call(bf16[2,128,768]{2,1,0:T(8,128)(2,1)} %xs_own.1, bf16[2,256,768]{2,1,0:T(8,128)(2,1)} %xl_own.1, ...), custom_call_target="tpu_custom_call" | custom-call | tf_op jit(solution)/shard_map/pallas_call | solution.py:1708
  297.6 5.7 %shard_map.189 = (bf16[2,128,768]{2,1,0:T(8,128)(2,1)}, bf16[2,256,768]{2,1,0:T(8,128)(2,1)}, f32[2,128,768]{2,1,0:T(8,128)}, f32[2,256,768]{2,1,0:T(8,128)}, f3...) custom-call(bf16[2,128,768]{2,1,0:T(8,128)(2,1)} %get-tuple-element., ...), custom_call_target="tpu_custom_call" | custom-call | tf_op jit(solution)/shard_map/pallas_call | solution.py:1769
where the time goes:
time: 309 us; the launch traced here: 304 us
  Pallas kernels  303 us (98%)
    pallas_call x1, Pallas kernels, first_part(): pl.pallas_call(first_kernel, out_shape=tuple((out(*one) for one in outs))...  129 us
    pallas_call x1, Pallas kernels, third_part(): pl.pallas_call(third_kernel, out_shape=(out(x_short.shape, F32), out(x_lo...  122 us
    pallas_call x1, Pallas kernels, second_part(): pl.pallas_call(second_kernel, out_shape=(out(x_short.shape, BF16), out(x_...  45.3 us

commit v1 on v0

--- a/solution.py
+++ b/solution.py
@@ -913,6 +913,7 @@
     project_long(0)
     rows_long.whole(1)
     project_long(1)
+    up_w.over()
     rows_long.whole(2)
     project_long(2)
     rows_short.step(0)
@@ -928,8 +929,8 @@
     project_short(3)
     rows_long.whole(3)
     project_long(3)
-    up_w.over()
     out_w.over()
+    up_w.turn()
     conv_short()
     attend_short(0)
     send_short(0)
@@ -944,15 +945,14 @@
     save_long()
     attend_long(0)
     send_long(0)
-    up_w.turn()
     attend_long(4)
     send_long(4)
     out_w.turn()
+    down_w.over()
     attend_long(1)
     send_long(1)
     attend_long(5)
     send_long(5)
-    down_w.over()
     up_w.last()
     out_w.last()
     attend_long(2)

time: 309 us -> 305 us (0.987)
  Pallas kernels: 303 us -> 298 us
where the time goes in v1:
time: 305 us; the launch traced here: 299 us
  Pallas kernels  298 us (98%)
    pallas_call x1, Pallas kernels, first_part(): pl.pallas_call(first_kernel, out_shape=tuple((out(*one) for one in outs))...  126 us
    pallas_call x1, Pallas kernels, third_part(): pl.pallas_call(third_kernel, out_shape=(out(x_short.shape, F32), out(x_lo...  121 us
    pallas_call x1, Pallas kernels, second_part(): pl.pallas_call(second_kernel, out_shape=(out(x_short.shape, BF16), out(x_...  45.1 us

profile of v1, /device:TPU:0, one launch (start us, length us, event | category | flops | bytes accessed | tf_op | source)
XLA Modules:
  0.0 299.3 jit_solution(4514620801256487787)
XLA Ops:
  0.6 126.2 %shard_map.186 = (bf16[768,768]{1,0:T(8,128)(2,1)}, bf16[4,2,2,2,24,768]{5,4,3,2,1,0:T(8,128)(2,1)}, bf16[4,2,2,2,24,3072]{5,4,3,2,1,0:T(8,128)(2,1)}, bf16[4,2,...) custom-call(s32[2,2]{1,0:T(2,128)} %lens.1, ...), custom_call_target="tpu_custom_call" | custom-call | tf_op jit(solution)/shard_map/pallas_call | solution.py:1052
  126.8 45.1 %shard_map.187 = (bf16[2,128,768]{2,1,0:T(8,128)(2,1)}, bf16[2,256,768]{2,1,0:T(8,128)(2,1)}, f32[768,768]{1,0:T(8,128)}, f32[8,768]{1,0:T(8,128)}, bf16[4,2,2,2...) custom-call(bf16[2,128,768]{2,1,0:T(8,128)(2,1)} %xs_own.1, ...), custom_call_target="tpu_custom_call" | custom-call | tf_op jit(solution)/shard_map/pallas_call | solution.py:1238
  172.0 121.4 %shard_map.188 = (f32[2,128,768]{2,1,0:T(8,128)}, f32[2,256,768]{2,1,0:T(8,128)}, f32[24,2304]{1,0:T(8,128)}, f32[24,768]{1,0:T(8,128)}, f32[24,3072]{1,0:T(8,12...) custom-call(bf16[2,128,768]{2,1,0:T(8,128)(2,1)} %xs_own.1, bf16[2,256,768]{2,1,0:T(8,128)(2,1)} %xl_own.1, ...), custom_call_target="tpu_custom_call" | custom-call | tf_op jit(solution)/shard_map/pallas_call | solution.py:1708
  293.4 5.7 %shard_map.189 = (bf16[2,128,768]{2,1,0:T(8,128)(2,1)}, bf16[2,256,768]{2,1,0:T(8,128)(2,1)}, f32[2,128,768]{2,1,0:T(8,128)}, f32[2,256,768]{2,1,0:T(8,128)}, f3...) custom-call(bf16[2,128,768]{2,1,0:T(8,128)(2,1)} %get-tuple-element., ...), custom_call_target="tpu_custom_call" | custom-call | tf_op jit(solution)/shard_map/pallas_call | solution.py:1769
